TPU v7x, 768 devices: a whole 4x8x12 slice. The times are simulated.
768 devices in a mesh: segment: 4 (over y_hi, core), lane: 4 (over x), dp: 48 (over y_lo, z).
Axes of the slice: x: 4, y: 8 (y_hi: 2, y_lo: 4; y = y_hi * 4 + y_lo), z: 12, core: 2. Of those that a mesh axis runs over, the one named last changes fastest.
Arguments:
- inputs: bfloat16 [4, 2, 3072, 3072], P('segment', None, 'dp', 'lane'), may hold values from -6 to 6
- gate_sums: bfloat16 [4, 2, 3072, 3264], P('segment', None, 'dp', 'lane'), may hold values from -6 to 6
- top_grads: bfloat16 [2, 3072, 3072], P(None, 'dp', 'lane'), may hold values from -6 to 6
- up_weight: bfloat16 [4, 3072, 3264], P('segment', None, 'lane'), may hold values from -0.109375 to 0.109375
- down_weight: bfloat16 [4, 3264, 3072], P('segment', 'lane'), may hold values from -0.109375 to 0.109375
- projectors: bfloat16 [4, 2, 3264, 128], P('segment', None, 'lane'), may hold values from -1 to 1, as said below
- first_moment: float32 [4, 4, 2, 128, 3072], P('segment', 'lane', None, None, 'dp'), may hold values from -48 to 48
- second_moment: float32 [4, 4, 2, 128, 3072], P('segment', 'lane', None, None, 'dp'), may hold values from 122.88 to 3072
Outputs:
- input_grads: bfloat16 [4, 2, 3072, 3072], P('segment', None, 'dp', 'lane')
- new_first: float32 [4, 4, 2, 128, 3072], P('segment', 'lane', None, None, 'dp')
- new_second: float32 [4, 4, 2, 128, 3072], P('segment', 'lane', None, None, 'dp')
- new_up: bfloat16 [4, 3072, 3264], P('segment', 'dp', 'lane')
- new_down: bfloat16 [4, 3264, 3072], P('segment', 'lane', 'dp')
Inputs may be any that keep to these rules, and one draw needn't show every extreme that they name: For every section, kind and lane, the 816 rows of projectors that belong to that lane form a matrix with orthonormal columns, up to bfloat16 rounding.
All inputs are finite; a program needn't handle non-finite values.
Results may differ from a plain program's by a relative error of at most 0.018.
Values may be sent and summed in bfloat16 or wider, within the bound.
A program may use at most 64 MiB of HBM per device.

v0:
```python
import jax
import jax.numpy as jnp
from jax import lax
from jax.sharding import PartitionSpec as P


def shifted(value, axis, by):
    size = lax.axis_size(axis)
    pairs = [(i, i + by) for i in range(size) if 0 <= i + by < size]
    return lax.ppermute(value, axis, pairs)


def code_terms(codes_up, codes_down, rows_in, rows_cot):
    merged_up = jnp.concatenate(codes_up, axis=0)
    merged_down = jnp.concatenate(codes_down, axis=0)
    merged_in = jnp.concatenate(rows_in, axis=0)
    merged_cot = jnp.concatenate(rows_cot, axis=0)
    contract_rows = (((0,), (0,)), ((), ()))
    term_up = lax.dot_general(
        merged_up, merged_in, contract_rows, preferred_element_type=jnp.float32
    )
    term_down = lax.dot_general(
        merged_down, merged_cot, contract_rows, preferred_element_type=jnp.float32
    )
    return jnp.stack([term_up, term_down])


def local(
    inputs, gate_sums, top_grads, up_weight, down_weight, projectors, first_moment, second_moment
):
    segment_count = lax.axis_size("segment")
    segment_index = lax.axis_index("segment")
    micro_count = inputs.shape[1]
    row_count = inputs.shape[2]
    weight_up = up_weight[0]
    weight_down = down_weight[0]
    proj_up = projectors[0, 0]
    proj_down = projectors[0, 1]
    rank_count = proj_up.shape[1]
    contract_cols = (((1,), (1,)), ((), ()))
    inputs_full = lax.all_gather(inputs[0], "lane", axis=2, tiled=True)
    full_width = inputs_full.shape[2]
    slice_width = first_moment.shape[4]
    offset = lax.axis_index("dp") * slice_width
    received = jnp.zeros_like(top_grads[0])
    outgrads = jnp.zeros_like(inputs[0])
    tick_count = micro_count + segment_count - 1
    codes_up = []
    codes_down = []
    rows_in = []
    rows_cot = []
    for tick_index in range(tick_count):
        micro_index = tick_index - (segment_count - 1 - segment_index)
        active = (micro_index >= 0) & (micro_index < micro_count)
        picked = jnp.clip(micro_index, 0, micro_count - 1)
        top_piece = lax.dynamic_index_in_dim(top_grads, picked, 0, keepdims=False)
        incoming = jnp.where(segment_index == segment_count - 1, top_piece, received)
        cotangent = lax.all_gather(incoming, "lane", axis=1, tiled=True)
        input_rows = lax.dynamic_index_in_dim(inputs_full, picked, 0, keepdims=False)

        def active_work():
            gate_rows = lax.dynamic_index_in_dim(gate_sums[0], picked, 0, keepdims=False)
            up_value = jnp.dot(input_rows, weight_up, preferred_element_type=jnp.float32)
            gate_act = jax.nn.silu(gate_rows.astype(jnp.float32))
            hidden = (gate_act * up_value).astype(jnp.bfloat16)
            hidden_grad = lax.dot_general(
                cotangent, weight_down, contract_cols, preferred_element_type=jnp.float32
            )
            up_grad = (hidden_grad * gate_act).astype(jnp.bfloat16)
            partial_value = lax.dot_general(
                up_grad, weight_up, contract_cols, preferred_element_type=jnp.float32
            )
            code_up = jnp.dot(up_grad, proj_up, preferred_element_type=jnp.float32).astype(
                jnp.bfloat16
            )
            code_down = jnp.dot(hidden, proj_down, preferred_element_type=jnp.float32).astype(
                jnp.bfloat16
            )
            return (partial_value, code_up, code_down)

        def spare_work():
            blank = jnp.zeros((row_count, rank_count), jnp.bfloat16)
            return (jnp.zeros((row_count, full_width), jnp.float32), blank, blank)

        partial_value, code_up, code_down = lax.cond(active, active_work, spare_work)
        codes_up.append(code_up)
        codes_down.append(code_down)
        rows_in.append(input_rows)
        rows_cot.append(cotangent)
        shares = lax.psum_scatter(
            partial_value.astype(jnp.bfloat16), "lane", scatter_dimension=1, tiled=True
        ).astype(jnp.float32)
        grad_input = (shares + incoming.astype(jnp.float32)).astype(jnp.bfloat16)
        updated = lax.dynamic_update_index_in_dim(outgrads, grad_input, picked, 0)
        outgrads = jnp.where(active, updated, outgrads)
        received = shifted(grad_input, "segment", -1)
    code_sums = code_terms(codes_up, codes_down, rows_in, rows_cot)
    owned = lax.psum_scatter(code_sums, "dp", scatter_dimension=2, tiled=True)
    first_next = 0.9 * first_moment[0, 0] + 0.1 * owned
    second_next = 0.999 * second_moment[0, 0] + 0.001 * owned * owned
    step_code = first_next / (jnp.sqrt(second_next) + 1e-08)
    up_rows = lax.dynamic_slice_in_dim(weight_up, offset, slice_width, 0)
    delta_up = lax.dot_general(
        step_code[0],
        proj_up.astype(jnp.float32),
        (((0,), (1,)), ((), ())),
        precision=lax.Precision.HIGHEST,
    )
    up_next = (up_rows.astype(jnp.float32) - 0.05 * delta_up).astype(jnp.bfloat16)
    down_cols = lax.dynamic_slice_in_dim(weight_down, offset, slice_width, 1)
    delta_down = jnp.dot(
        proj_down.astype(jnp.float32), step_code[1], precision=lax.Precision.HIGHEST
    )
    down_next = (down_cols.astype(jnp.float32) - 0.05 * delta_down).astype(jnp.bfloat16)
    return (
        outgrads[None],
        first_next[None, None],
        second_next[None, None],
        up_next[None],
        down_next[None],
    )


def solution(mesh):
    placed = (
        P("segment", None, "dp", "lane"),
        P("segment", None, "dp", "lane"),
        P(None, "dp", "lane"),
        P("segment", None, "lane"),
        P("segment", "lane", None),
        P("segment", None, "lane", None),
        P("segment", "lane", None, None, "dp"),
        P("segment", "lane", None, None, "dp"),
    )
    return jax.shard_map(
        local,
        mesh=mesh,
        in_specs=placed,
        out_specs=(
            P("segment", None, "dp", "lane"),
            P("segment", "lane", None, None, "dp"),
            P("segment", "lane", None, None, "dp"),
            P("segment", "dp", "lane"),
            P("segment", "lane", "dp"),
        ),
        check_vma=False,
    )
```

profile of v0, /device:TPU:6, one launch (start us, length us, event | category | flops | bytes accessed | tf_op | source)
XLA Modules:
  0.0 789.1 jit_solution(3575729316862761053)
XLA Ops:
  8.1 19.1 %all-gather = bf16[1,64,3072]{2,1,0:T(8,128)(2,1)S(1)} all-gather(bf16[1,64,768]{2,1,0:T(8,128)(2,1)S(1)} %dynamic-slice_select_fusion), channel_id=2, replica_groups=mesh['segment'=4,'lane'=4,'dp'=48] {'lane'}, dimensions={2}, use_global_device_ids=true | all-gather | bytes 491520 | tf_op jit(solution)/shard_map/all_gather | solution.py:58
  27.3 14.0 %all-gather.1 = bf16[1,2,64,3072]{3,2,1,0:T(8,128)(2,1)S(1)} all-gather(bf16[1,2,64,768]{3,2,1,0:T(8,128)(2,1)} %param.18), channel_id=3, replica_groups=mesh['segment'=4,'lane'=4,'dp'=48] {'lane'}, dimensions={3}, use_global_device_ids=true | all-gather | bytes 983040 | tf_op jit(solution)/shard_map/all_gather | solution.py:41
  42.1 7.7 copy.20
  51.7 31.5 %reduce-scatter.6.cloned.1.call-done = bf16[64,768]{1,0:T(8,128)(2,1)} async-done(((bf16[64,3072]{1,0:T(8,128)(2,1)}), bf16[64,768]{1,0:T(8,128)(2,1)}) %reduce-scatter.6.cloned.1.call-update) | async-done | bytes 98320 | tf_op jit(solution)/shard_map/reduce_scatter | solution.py:90
  84.1 1.3 collective-permute-start
  87.3 12.5 %all_gather.20 = bf16[64,3072]{1,0:T(8,128)(2,1)S(1)} all-gather(bf16[64,768]{1,0:T(8,128)(2,1)S(1)} %bitcast_select_fusion.6), channel_id=1, replica_groups=mesh['segment'=4,'lane'=4,'dp'=48] {'lane'}, dimensions={1}, use_global_device_ids=true | all-gather | bytes 491520 | tf_op jit(solution)/shard_map/all_gather | solution.py:58
  102.4 38.5 %reduce-scatter.8.cloned.1.call-done = bf16[64,768]{1,0:T(8,128)(2,1)} async-done(((bf16[64,3072]{1,0:T(8,128)(2,1)}), bf16[64,768]{1,0:T(8,128)(2,1)}) %reduce-scatter.8.cloned.1.call-update) | async-done | bytes 98320 | tf_op jit(solution)/shard_map/reduce_scatter | solution.py:90
  141.8 1.3 collective-permute-start.1
  145.1 12.5 %all_gather.21 = bf16[64,3072]{1,0:T(8,128)(2,1)S(1)} all-gather(bf16[64,768]{1,0:T(8,128)(2,1)S(1)} %bitcast_select_fusion.4), channel_id=1, replica_groups=mesh['segment'=4,'lane'=4,'dp'=48] {'lane'}, dimensions={1}, use_global_device_ids=true | all-gather | bytes 491520 | tf_op jit(solution)/shard_map/all_gather | solution.py:58
  159.3 39.2 %reduce-scatter.10.cloned.1.call-done = bf16[64,768]{1,0:T(8,128)(2,1)} async-done(((bf16[64,3072]{1,0:T(8,128)(2,1)}), bf16[64,768]{1,0:T(8,128)(2,1)}) %reduce-scatter.10.cloned.1.call-update) | async-done | bytes 98320 | tf_op jit(solution)/shard_map/reduce_scatter | solution.py:90
  199.5 1.5 collective-permute-start.2
  201.0 1.7 collective-permute-done.2
  202.7 12.5 %all_gather.22 = bf16[64,3072]{1,0:T(8,128)(2,1)S(1)} all-gather(bf16[64,768]{1,0:T(8,128)(2,1)S(1)} %bitcast_select_fusion.2), channel_id=1, replica_groups=mesh['segment'=4,'lane'=4,'dp'=48] {'lane'}, dimensions={1}, use_global_device_ids=true | all-gather | bytes 491520 | tf_op jit(solution)/shard_map/all_gather | solution.py:58
  215.2 9.9 %conditional.8 = (bf16[64,3072]{1,0:T(8,128)(2,1)S(1)}, bf16[64,128]{1,0:T(8,128)(2,1)S(1)}, bf16[64,128]{1,0:T(8,128)(2,1)S(1)}) conditional(s32[]{:T(128)} %convert_element_type.200, () %tuple.54, (bf16[64,3072]{1,0:T(8,128)(2,1)S(1)}, bf16[816,3072]{1,0:T(8,128)(2,1)}, s32[]{:T(128)}, bf16[1,2,64,816]{3,2,1,0:T(8,128)(2,1)S(1)}, ...), branch_computations={%region_9.10_spmd, %region_10.11_spmd} | conditional | flops 990078976 | bytes 37257312 | solution.py:85
  215.2 4.2 fusion.27
  219.5 1.8 fusion.69
  221.4 3.7 fusion.30
  227.5 27.3 %reduce-scatter.12.cloned.1.call-done = bf16[64,768]{1,0:T(8,128)(2,1)} async-done(((bf16[64,3072]{1,0:T(8,128)(2,1)}), bf16[64,768]{1,0:T(8,128)(2,1)}) %reduce-scatter.12.cloned.1.call-update) | async-done | bytes 98320 | tf_op jit(solution)/shard_map/reduce_scatter | solution.py:90
  255.8 1.3 collective-permute-start.3
  257.1 1.9 collective-permute-done.3
  259.0 12.5 %all_gather.23 = bf16[64,3072]{1,0:T(8,128)(2,1)S(1)} all-gather(bf16[64,768]{1,0:T(8,128)(2,1)S(1)} %bitcast_select_fusion), channel_id=1, replica_groups=mesh['segment'=4,'lane'=4,'dp'=48] {'lane'}, dimensions={1}, use_global_device_ids=true | all-gather | bytes 491520 | tf_op jit(solution)/shard_map/all_gather | solution.py:58
  272.3 9.9 %conditional.9 = (bf16[64,3072]{1,0:T(8,128)(2,1)S(1)}, bf16[64,128]{1,0:T(8,128)(2,1)S(1)}, bf16[64,128]{1,0:T(8,128)(2,1)S(1)}) conditional(s32[]{:T(128)} %convert_element_type.205, () %tuple.56, (bf16[64,3072]{1,0:T(8,128)(2,1)S(1)}, bf16[816,3072]{1,0:T(8,128)(2,1)}, s32[]{:T(128)}, bf16[1,2,64,816]{3,2,1,0:T(8,128)(2,1)S(1)}, ...), branch_computations={%region_12.13_spmd, %region_13.14_spmd} | conditional | flops 990078976 | bytes 37257312 | solution.py:85
  272.3 4.2 fusion.36
  276.5 1.8 fusion.70
  278.5 3.7 fusion.39
  283.1 2.1 convolution_bitcast_fusion.1
  286.1 3.4 copy.22
  289.5 1.1 constant_dynamic-slice_fusion
  290.8 1.3 dynamic-slice.22
  293.6 16.6 %reduce-scatter.14.cloned.1.call-done = bf16[64,768]{1,0:T(8,128)(2,1)} async-done(((bf16[64,3072]{1,0:T(8,128)(2,1)}), bf16[64,768]{1,0:T(8,128)(2,1)}) %reduce-scatter.14.cloned.1.call-update) | async-done | bytes 98320 | tf_op jit(solution)/shard_map/reduce_scatter | solution.py:90
  311.2 465.9 %all-reduce.3.cloned.1.call-done = f32[2,128,3072]{1,0,2:T(2,128)} async-done(((f32[2,128,3072]{1,0,2:T(2,128)}), f32[2,128,3072]{1,0,2:T(2,128)}) %all-reduce.3.cloned.1.call-update) | async-done | bytes 3145744
  778.1 1.9 fusion.51
  (93 shorter events, 27.5 us)
Async XLA Ops:
  7.2 76.0 %reduce-scatter.6.cloned.1.call-start = ((), (), s32[]{:S(2)}) async-start(), calls=%async_computation.5 | async-start | bytes 491520 | tf_op jit(solution)/shard_map/reduce_scatter | solution.py:90
  42.1 7.8 copy-start.8
  42.1 7.8 copy-start.5
  49.9 33.3 %copy-start.7 = (bf16[2,64,768]{2,1,0:T(8,128)(2,1)S(1)}, bf16[2,64,768]{2,1,0:T(8,128)(2,1)}, u32[]{:S(2)}) copy-start(bf16[2,64,768]{2,1,0:T(8,128)(2,1)} %param.20) | copy-start | bytes 589828
  50.0 0.8 copy-start.11
  50.8 90.1 %reduce-scatter.8.cloned.1.call-start = ((), (), s32[]{:S(2)}) async-start(), calls=%async_computation.6 | async-start | bytes 491520 | tf_op jit(solution)/shard_map/reduce_scatter | solution.py:90
  84.1 3.2 collective-permute-start
  100.7 97.8 %reduce-scatter.10.cloned.1.call-start = ((), (), s32[]{:S(2)}) async-start(), calls=%async_computation.7 | async-start | bytes 491520 | tf_op jit(solution)/shard_map/reduce_scatter | solution.py:90
  141.8 3.2 collective-permute-start.1
  158.4 96.4 %reduce-scatter.12.cloned.1.call-start = ((), (), s32[]{:S(2)}) async-start(), calls=%async_computation.8 | async-start | bytes 491520 | tf_op jit(solution)/shard_map/reduce_scatter | solution.py:90
  199.5 3.2 collective-permute-start.2
  215.2 4.3 copy-start.3
  225.1 0.7 copy-start.12
  225.9 84.3 %reduce-scatter.14.cloned.1.call-start = ((), (), s32[]{:S(2)}) async-start(), calls=%async_computation.9 | async-start | bytes 491520 | tf_op jit(solution)/shard_map/reduce_scatter | solution.py:90
  255.8 3.2 collective-permute-start.3
  272.3 4.3 copy-start.4
  282.2 0.8 copy-start.13
  282.2 3.0 copy-start.6
  283.0 494.0 %all-reduce.3.cloned.1.call-start = ((), (), s32[]{:S(2)}) async-start(), calls=%async_computation.10 | async-start | bytes 6291456
  286.1 6.6 copy-start.15
  289.5 488.7 %copy-start.9 = (bf16[1,2,816,128]{3,2,1,0:T(8,128)(2,1)S(1)}, bf16[1,2,816,128]{3,2,1,0:T(8,128)(2,1)}, u32[]{:S(2)}) copy-start(bf16[1,2,816,128]{3,2,1,0:T(8,128)(2,1)} %param.23) | copy-start | bytes 1253380
  311.2 471.1 %copy-start.14 = (bf16[1,2,64,768]{3,2,1,0:T(8,128)(2,1)}, bf16[1,2,64,768]{3,2,1,0:T(8,128)(2,1)S(1)}, u32[]{:S(2)}) copy-start(bf16[1,2,64,768]{3,2,1,0:T(8,128)(2,1)S(1)} %fusion.56) | copy-start | bytes 589828
Sparse Core Ops, SparseCore 0:
  50.9 32.2 reduce-scatter.5
  100.8 40.0 reduce-scatter.7
  158.5 39.9 reduce-scatter.9
  226.0 28.7 reduce-scatter.11
  283.1 27.0 reduce-scatter.13
  313.6 463.3 all-reduce.2
where the time goes:
time: 790 us; the launch traced here: 789 us
  waiting for transfers between devices  625 us (79%)
  blocking collectives  83.2 us (11%)
  local copies, waits for them, and re-layouts  27.2 us (3%)
  matrix products  25.5 us (3%)
  between operations  15.1 us (2%)
    unnamed x7, waiting for transfers between devices  466 us
    reduce_scatter x5, waiting for transfers between devices, local(): lax.psum_scatter(partial_value.astype(jnp.bfloat16), 'lane', scatter_dime...  153 us
    all_gather x5, blocking collectives, local(): cotangent = lax.all_gather(incoming, 'lane', axis=1, tiled=True)  69.2 us
    unnamed x41, local copies, waits for them, and re-layouts  19.4 us
  transfers between devices with their start and end apart: 10, of which 10 were waited for; matrix products, arithmetic and copies ran while one was open for 2% of the time, Pallas kernels for 0%

commit v1 on v0

v1 whole, which is shorter than its diff:
```python
import functools

import jax
import jax.numpy as jnp
from jax import lax
from jax.experimental import pallas as pl
from jax.experimental.pallas import tpu as pltpu
from jax.sharding import PartitionSpec as P

MESH = pl.DeviceIdType.MESH
NT = (((1,), (1,)), ((), ()))
NN = (((1,), (0,)), ((), ()))
TN = (((0,), (0,)), ((), ()))
BF = jnp.bfloat16
F32 = jnp.float32


def mm(a, b, dims):
    return lax.dot_general(a, b, dims, preferred_element_type=F32)


def kernel(
    zn,
    x_hbm, gate_hbm, top_hbm, wu_hbm, wd_hbm, proj_hbm, m1_hbm, m2_hbm,
    og_hbm, nf_hbm, ns_hbm, nu_hbm, nd_hbm,
    wu, wd, proj, gate, m1, m2,
    xg, cg, act, acc, ug, hid, part, prs, og,
    cup, cdn, terms, zsrc, zrecv, ysend, yrecv, ykeep,
    base, nfv, nsv, nwv,
    loc, wsem, out_sem,
    ag_s, bc_s, ag_r, yh_s, yh_r, in_s, in_r, rs_s, rs_r, z_s, z_r, y_s, y_r,
):
    s = lax.axis_index("segment")
    l = lax.axis_index("lane")
    dp = lax.axis_index("dp")
    z = lax.rem(dp, zn)
    y = dp // zn
    odd = lax.rem(s, 2) == 1
    pair = s + 1 - 2 * lax.rem(s, 2)

    def lane(k):
        return lax.rem(l + k, 4)

    def zdev(k):
        return y * zn + lax.rem(z + k + zn, zn)

    def ydev(k):
        return lax.rem(y + k, 4) * zn + z

    loads = [
        pltpu.make_async_copy(gate_hbm, gate, loc.at[0]),
        pltpu.make_async_copy(x_hbm, xg.at[l], loc.at[1]),
        pltpu.make_async_copy(proj_hbm, proj, loc.at[2]),
        pltpu.make_async_copy(m1_hbm, m1, loc.at[3]),
        pltpu.make_async_copy(m2_hbm, m2, loc.at[4]),
    ]
    wd_loads = [
        pltpu.make_async_copy(wd_hbm.at[:, pl.ds(kb * 768, 768)], wd.at[kb], wsem.at[0, kb])
        for kb in range(4)
    ]
    wu_loads = [
        pltpu.make_async_copy(wu_hbm.at[:, pl.ds(kb * 768, 768)], wu.at[kb], wsem.at[1, kb])
        for kb in range(4)
    ]
    top_load = pltpu.make_async_copy(top_hbm, cg.at[l], loc.at[5])

    @pl.when(s == 3)
    def _():
        top_load.start()

    for c in wd_loads + wu_loads + loads:
        c.start()

    barrier = pltpu.get_barrier_semaphore()

    def greet(dev):
        pl.semaphore_signal(barrier, inc=1, device_id=dev, device_id_type=MESH)

    for k in (1, 2, 3):
        greet({"lane": lane(k)})
        greet({"dp": ydev(k)})
    for k in range(4):
        greet({"segment": pair, "lane": lane(k)})
    greet({"segment": 3 - s})
    greet({"dp": zdev(1)})
    greet({"dp": zdev(-1)})
    pl.semaphore_wait(barrier, 13)

    def remote(src, dst, ss, rr, dev):
        return pltpu.make_async_remote_copy(
            src_ref=src, dst_ref=dst, send_sem=ss, recv_sem=rr, device_id=dev, device_id_type=MESH
        )

    def gather_top(u, k):
        return remote(top_hbm.at[u], cg.at[l, u], ag_s.at[u, k], ag_r.at[u, k], {"lane": lane(k)})

    def gather_cot(u, k):
        return remote(cg.at[l, u], cg.at[l, u], ag_s.at[u, k], ag_r.at[u, k], {"lane": lane(k)})

    def gather_in(k):
        return remote(x_hbm, xg.at[l], in_s.at[k], in_r.at[k], {"lane": lane(k)})

    def cast_down(u, k):
        return remote(
            og.at[u], cg.at[l, u], bc_s.at[u, k], ag_r.at[u, k], {"segment": pair, "lane": lane(k)}
        )

    def hop(u):
        return remote(og.at[u], cg.at[l, u], yh_s.at[u], yh_r.at[u], {"segment": 3 - s})

    def scatter(u, k):
        return remote(part.at[u, k], prs.at[u, k], rs_s.at[u, k], rs_r.at[u, k], {"lane": lane(k)})

    ORDER = (2, 1, 3)

    @pl.when(s == 3)
    def _():
        for u in range(2):
            for k in ORDER:
                gather_top(u, k).start()

    for c in loads:
        c.wait()
    v = gate[...].reshape(128, 816).astype(F32)
    act[...] = v / (1.0 + jnp.exp(-v))

    for c in wd_loads:
        c.wait()
    for c in wu_loads:
        c.wait()

    for k in ORDER:
        gather_in(k).start()

    @pl.when(s == 3)
    def _():
        top_load.wait()

    pick = lax.broadcasted_iota(jnp.int32, (64, 128), 0) + 64 * lax.rem(z, 2)
    pick = (lax.broadcasted_iota(jnp.int32, (64, 128), 1) == pick).astype(BF)
    at = pl.ds(pl.multiple_of((z // 2) * 128, 128), 128)
    base[0] = mm(pick, wu[y, :, at], NT)
    base[1] = mm(pick, wd[y, :, at], NT)

    def prep():
        for k in (0, 1, 3, 2):
            kb = lane(4 - k)
            if k:
                gather_in(k).wait_recv()
            r = mm(xg[kb].reshape(128, 768), wu[kb], NT)
            if k == 0:
                acc[...] = r
            else:
                acc[...] += r
        hid[...] = (acc[...] * act[...]).astype(BF)
        cdn[...] = mm(hid[...], proj[1], NN).astype(BF)

    @pl.when(s < 3)
    def _():
        prep()

    def first(u):
        rows = slice(u * 64, u * 64 + 64)

        @pl.when(s == 1)
        def _():
            hop(u).wait_recv()
            for k in ORDER:
                gather_cot(u, k).start()

        for k in (0, 1, 3, 2):
            kb = lane(4 - k)
            if k:
                gather_cot(u, k).wait_recv()
            else:
                @pl.when(jnp.logical_not(odd))
                def _():
                    cast_down(u, 0).wait_recv()
            r = mm(cg[kb, u], wd[kb], NT)
            if k == 0:
                acc[0:64, :] = r
            else:
                acc[0:64, :] += r
        ug[rows, :] = (acc[0:64, :] * act[rows, :]).astype(BF)

    def second(u):
        rows = slice(u * 64, u * 64 + 64)
        for k in (2, 1, 3, 0):
            part[u, k] = mm(ug[rows, :], wu[lane(k)], NN).astype(BF)
            if k:
                scatter(u, k).start()

    def finish(u):
        total = cg[l, u].astype(F32) + part[u, 0].astype(F32)
        for k in (1, 3, 2):
            scatter(u, k).wait_recv()
            total += prs[u, k].astype(F32)
        og[u] = total.astype(BF)

        @pl.when(odd)
        def _():
            for k in (2, 1, 3, 0):
                cast_down(u, k).start()

        @pl.when(s == 2)
        def _():
            hop(u).start()

        pltpu.make_async_copy(og.at[u], og_hbm.at[u], out_sem.at[u]).start()

    def zcount(t, d):
        return 6 if t == d else 5

    def owner(n, d, k):
        return lax.rem(z + (n - k if d else k - n) + zn, zn)

    def zcopy(t, d, k):
        src = zsrc.at[t, d] if k == 0 else zrecv.at[t, d, k - 1]
        return remote(
            src, zrecv.at[t, d, k], z_s.at[t, d, k], z_r.at[t, d, k], {"dp": zdev(1 if d else -1)}
        )

    def ring_start(t):
        for d in range(2):
            zsrc[t, d] = terms[t, :, owner(zcount(t, d), d, 0)].astype(BF)
            zcopy(t, d, 0).start()

    def ring_step(t, k):
        for d in range(2):
            n = zcount(t, d)
            if k < n:
                zcopy(t, d, k - 1).wait_recv()
                mine = terms[t, :, owner(n, d, k)]
                zrecv[t, d, k - 1] = (zrecv[t, d, k - 1].astype(F32) + mine).astype(BF)
                zcopy(t, d, k).start()

    def make_term(t):
        rows_of, code = (xg, cup) if t == 0 else (cg, cdn)
        for kb in range(4):
            r = mm(rows_of[kb].reshape(128, 768), code[...], TN)
            terms[t, kb] = r.reshape(zn, 64, 128)

    def codes():
        cup[...] = mm(ug[...], proj[0], NN).astype(BF)
        for t in range(2):
            make_term(t)
            ring_start(t)

    first(0)
    second(0)
    first(1)

    @pl.when(s == 0)
    def _():
        finish(0)
        codes()

    second(1)

    @pl.when(s > 0)
    def _():
        finish(0)
        finish(1)

        @pl.when(s == 3)
        def _():
            prep()

        codes()

    for k in range(1, 6):
        for t in range(2):
            ring_step(t, k)
        if k == 3:
            @pl.when(s == 0)
            def _():
                finish(1)

    def ycopy(t, k):
        return remote(
            ysend.at[t, k], yrecv.at[t, k], y_s.at[t, k], y_r.at[t, k], {"dp": ydev(k)}
        )

    for t in range(2):
        for d in range(2):
            zcopy(t, d, zcount(t, d) - 1).wait_recv()
        for k in (3, 2, 1, 0):
            yo = lax.rem(y + k, 4)
            r = terms[t, yo, z]
            for d in range(2):
                r += zrecv[t, d, zcount(t, d) - 1, yo].astype(F32)
            if k:
                ysend[t, k] = r.astype(BF)
                ycopy(t, k).start()
            else:
                ykeep[t] = r

    outs = []
    for t in range(2):
        grad = ykeep[t]
        for k in (1, 2, 3):
            ycopy(t, k).wait_recv()
            grad += yrecv[t, k].astype(F32)
        new_first = 0.9 * m1[t] + 0.1 * grad
        new_second = 0.999 * m2[t] + 0.001 * grad * grad
        nfv[t] = new_first
        nsv[t] = new_second
        step = new_first / (jnp.sqrt(new_second) + 1e-08)
        high = step.astype(BF)
        low = (step - high.astype(F32)).astype(BF)
        delta = mm(high, proj[t], NT) + mm(low, proj[t], NT)
        nwv[t] = (base[t] - 0.05 * delta).astype(BF)
        outs += [
            pltpu.make_async_copy(nfv.at[t], nf_hbm.at[t], out_sem.at[2 + 3 * t]),
            pltpu.make_async_copy(nsv.at[t], ns_hbm.at[t], out_sem.at[3 + 3 * t]),
            pltpu.make_async_copy(nwv.at[t], (nu_hbm, nd_hbm)[t], out_sem.at[4 + 3 * t]),
        ]
        for c in outs[-3:]:
            c.start()

    @pl.when(s == 3)
    def _():
        for u in range(2):
            for k in ORDER:
                gather_top(u, k).wait_send()

    @pl.when(s == 1)
    def _():
        for u in range(2):
            for k in ORDER:
                gather_cot(u, k).wait_send()

    @pl.when(odd)
    def _():
        for u in range(2):
            for k in range(4):
                cast_down(u, k).wait_send()

    @pl.when(s == 2)
    def _():
        for u in range(2):
            hop(u).wait_send()

    for k in ORDER:
        gather_in(k).wait_send()
        for u in range(2):
            scatter(u, k).wait_send()
            ycopy(u, k).wait_send()
    for t in range(2):
        for d in range(2):
            for k in range(zcount(t, d)):
                zcopy(t, d, k).wait_send()
    for u in range(2):
        pltpu.make_async_copy(og.at[u], og_hbm.at[u], out_sem.at[u]).wait()
    for c in outs:
        c.wait()


def local(zn, inputs, gate_sums, top_grads, up_weight, down_weight, projectors, first_moment, second_moment):
    sds = jax.ShapeDtypeStruct
    any_spec = pl.BlockSpec(memory_space=pl.ANY)
    dma = pltpu.SemaphoreType.DMA
    og, nf, ns, nu, nd = pl.pallas_call(
        functools.partial(kernel, zn),
        out_shape=(
            sds((2, 64, 768), BF),
            sds((2, 64, 128), F32),
            sds((2, 64, 128), F32),
            sds((64, 816), BF),
            sds((64, 816), BF),
        ),
        in_specs=[any_spec] * 8,
        out_specs=(any_spec,) * 5,
        scratch_shapes=[
            pltpu.VMEM((4, 816, 768), BF),
            pltpu.VMEM((4, 816, 768), BF),
            pltpu.VMEM((2, 816, 128), BF),
            pltpu.VMEM((2, 64, 816), BF),
            pltpu.VMEM((2, 64, 128), F32),
            pltpu.VMEM((2, 64, 128), F32),
            pltpu.VMEM((4, 2, 64, 768), BF),
            pltpu.VMEM((4, 2, 64, 768), BF),
            pltpu.VMEM((128, 816), F32),
            pltpu.VMEM((128, 816), F32),
            pltpu.VMEM((128, 816), BF),
            pltpu.VMEM((128, 816), BF),
            pltpu.VMEM((2, 4, 64, 768), BF),
            pltpu.VMEM((2, 4, 64, 768), BF),
            pltpu.VMEM((2, 64, 768), BF),
            pltpu.VMEM((128, 128), BF),
            pltpu.VMEM((128, 128), BF),
            pltpu.VMEM((2, 4, zn, 64, 128), F32),
            pltpu.VMEM((2, 2, 4, 64, 128), BF),
            pltpu.VMEM((2, 2, 6, 4, 64, 128), BF),
            pltpu.VMEM((2, 4, 64, 128), BF),
            pltpu.VMEM((2, 4, 64, 128), BF),
            pltpu.VMEM((2, 64, 128), F32),
            pltpu.VMEM((2, 64, 816), F32),
            pltpu.VMEM((2, 64, 128), F32),
            pltpu.VMEM((2, 64, 128), F32),
            pltpu.VMEM((2, 64, 816), BF),
            dma((6,)),
            dma((2, 4)),
            dma((8,)),
            dma((2, 4)),
            dma((2, 4)),
            dma((2, 4)),
            dma((2,)),
            dma((2,)),
            dma((4,)),
            dma((4,)),
            dma((2, 4)),
            dma((2, 4)),
            dma((2, 2, 6)),
            dma((2, 2, 6)),
            dma((2, 4)),
            dma((2, 4)),
        ],
        compiler_params=pltpu.CompilerParams(
            collective_id=0, has_side_effects=True, vmem_limit_bytes=60 * 2**20
        ),
        name="relay",
    )(
        inputs[0],
        gate_sums[0],
        top_grads,
        jnp.swapaxes(up_weight[0], 0, 1),
        down_weight[0],
        projectors[0],
        jnp.swapaxes(first_moment[0, 0], 1, 2),
        jnp.swapaxes(second_moment[0, 0], 1, 2),
    )
    return (
        og[None],
        jnp.swapaxes(nf, 1, 2)[None, None],
        jnp.swapaxes(ns, 1, 2)[None, None],
        nu[None],
        jnp.swapaxes(nd, 0, 1)[None],
    )


def solution(mesh):
    placed = (
        P("segment", None, "dp", "lane"),
        P("segment", None, "dp", "lane"),
        P(None, "dp", "lane"),
        P("segment", None, "lane"),
        P("segment", "lane", None),
        P("segment", None, "lane", None),
        P("segment", "lane", None, None, "dp"),
        P("segment", "lane", None, None, "dp"),
    )
    return jax.shard_map(
        functools.partial(local, mesh.shape["dp"] // 4),
        mesh=mesh,
        in_specs=placed,
        out_specs=(
            P("segment", None, "dp", "lane"),
            P("segment", "lane", None, None, "dp"),
            P("segment", "lane", None, None, "dp"),
            P("segment", "dp", "lane"),
            P("segment", "lane", "dp"),
        ),
        check_vma=False,
    )
```

time: 790 us -> 118 us (0.15)
  waiting for transfers between devices: 625 us -> 0 us
  Pallas kernels: 0 us -> 109 us
  blocking collectives: 83.2 us -> 0 us
  matrix products: 25.5 us -> 0 us
  local copies, waits for them, and re-layouts: 27.2 us -> 7.67 us
  between operations: 15.1 us -> 0.64 us
    unnamed x7 -> x0, waiting for transfers between devices: 466 us -> none
    reduce_scatter x5 -> x0, waiting for transfers between devices: 153 us -> none  [local(): lax.psum_scatter(partial_value.astype(jnp.bfloat16), 'lane', scatter_dime...]
    pallas_call x0 -> x1, Pallas kernels: none -> 109 us  [local(): pl.pallas_call(functools.partial(kernel, zn), out_shape=(sds((2, 64, 768)...]
    all_gather x6 -> x0, blocking collectives: 83.2 us -> none  [the longest x5 69.2 us: local(): cotangent = lax.all_gather(incoming, 'lane', axis=1, tiled=True)]
    dot_general x12 -> x0, matrix products: 25.5 us -> none  [the longest x2 8.49 us: active_work(): lax.dot_general(cotangent, weight_down, contract_cols, preferred_element_...]
    unnamed x41 -> x5, local copies, waits for them, and re-layouts: 19.4 us -> 7.67 us
  transfers between devices with their start and end apart: 10 -> 0, of which waited for: 10 -> 0; matrix products, arithmetic and copies ran while one was open for 2% -> 0% of each run, Pallas kernels for 0% -> 0%
where the time goes in v1:
time: 118 us; the launch traced here: 117 us
  Pallas kernels  109 us (92%)
  local copies, waits for them, and re-layouts  7.67 us (6%)
    pallas_call x1, Pallas kernels, local(): pl.pallas_call(functools.partial(kernel, zn), out_shape=(sds((2, 64, 768)...  109 us
    unnamed x5, local copies, waits for them, and re-layouts  7.67 us

profile of v1, /device:TPU:6, one launch (start us, length us, event | category | flops | bytes accessed | tf_op | source)
XLA Modules:
  0.0 117.3 jit_solution(15163016204758812755)
XLA Ops:
  0.6 108.9 %relay.1 = (bf16[2,64,768]{2,1,0:T(8,128)(2,1)}, f32[2,64,128]{2,1,0:T(8,128)}, f32[2,64,128]{2,1,0:T(8,128)}, bf16[64,816]{1,0:T(8,128)(2,1)}, bf16[64,816]{1,0:T(8,128)(2,1)}) custom-call(bf16[2,64,768]{2,1,0:T(8,128)(2,1)} %bitcast.29, bf16[2,64,816]{2,1,0:T(8,128)(2,1)} %bitcast.27, bf16[2,64,768]{2,1,0:T(8,128)(2,1)} %top_hbm.1, ...), custom_call_target="tpu_custom_call" | custom-call | tf_op jit(solution)/shard_map/relay/pallas_call | solution.py:363
  109.6 1.6 %copy.18 = bf16[1,2,64,768]{3,2,1,0:T(8,128)(2,1)} copy(bf16[1,2,64,768]{3,2,1,0:T(8,128)(2,1)} %bitcast.28) | data formatting | bytes 393216
  111.2 1.5 %copy.19 = f32[1,1,2,128,64]{3,4,2,1,0:T(8,128)} copy(f32[1,1,2,128,64]{3,4,2,1,0:T(8,128)} %bitcast.35) | data formatting | bytes 131072
  112.7 1.5 %copy.20 = f32[1,1,2,128,64]{3,4,2,1,0:T(8,128)} copy(f32[1,1,2,128,64]{3,4,2,1,0:T(8,128)} %bitcast.34) | data formatting | bytes 131072
  114.2 1.6 %copy.21 = bf16[1,64,816]{2,1,0:T(8,128)(2,1)} copy(bf16[1,64,816]{2,1,0:T(8,128)(2,1)} %bitcast.31) | data formatting | bytes 208896
  115.7 1.6 %copy.22 = bf16[1,816,64]{1,2,0:T(8,128)(2,1)} copy(bf16[1,816,64]{1,2,0:T(8,128)(2,1)} %bitcast.30) | data formatting | bytes 208896

commit v2 on v1

--- a/solution.py
+++ b/solution.py
@@ -1,3 +1,4 @@
+import contextlib
 import functools
 
 import jax
@@ -8,6 +9,7 @@
 from jax.sharding import PartitionSpec as P
 
 MESH = pl.DeviceIdType.MESH
+scope = contextlib.nullcontext
 NT = (((1,), (1,)), ((), ()))
 NN = (((1,), (0,)), ((), ()))
 TN = (((0,), (0,)), ((), ()))
@@ -22,12 +24,12 @@
 def kernel(
     zn,
     x_hbm, gate_hbm, top_hbm, wu_hbm, wd_hbm, proj_hbm, m1_hbm, m2_hbm,
-    og_hbm, nf_hbm, ns_hbm, nu_hbm, nd_hbm,
+    og, nfv, nsv, nup, ndown,
     wu, wd, proj, gate, m1, m2,
-    xg, cg, act, acc, ug, hid, part, prs, og,
+    xg, cg, act, acc, ug, hid, part, prs,
     cup, cdn, terms, zsrc, zrecv, ysend, yrecv, ykeep,
-    base, nfv, nsv, nwv,
-    loc, wsem, out_sem,
+    base,
+    loc, wsem,
     ag_s, bc_s, ag_r, yh_s, yh_r, in_s, in_r, rs_s, rs_r, z_s, z_r, y_s, y_r,
 ):
     s = lax.axis_index("segment")
@@ -84,7 +86,8 @@
     greet({"segment": 3 - s})
     greet({"dp": zdev(1)})
     greet({"dp": zdev(-1)})
-    pl.semaphore_wait(barrier, 13)
+    with scope("entry"):
+        pl.semaphore_wait(barrier, 13)
 
     def remote(src, dst, ss, rr, dev):
         return pltpu.make_async_remote_copy(
@@ -119,15 +122,17 @@
             for k in ORDER:
                 gather_top(u, k).start()
 
-    for c in loads:
-        c.wait()
-    v = gate[...].reshape(128, 816).astype(F32)
-    act[...] = v / (1.0 + jnp.exp(-v))
-
-    for c in wd_loads:
-        c.wait()
-    for c in wu_loads:
-        c.wait()
+    with scope("act"):
+        for c in loads:
+            c.wait()
+        v = gate[...].reshape(128, 816).astype(F32)
+        act[...] = v / (1.0 + jnp.exp(-v))
+
+    with scope("weights"):
+        for c in wd_loads:
+            c.wait()
+        for c in wu_loads:
+            c.wait()
 
     for k in ORDER:
         gather_in(k).start()
@@ -145,8 +150,9 @@
     def prep():
         for k in (0, 1, 3, 2):
             kb = lane(4 - k)
-            if k:
-                gather_in(k).wait_recv()
+            with scope("prepwait"):
+                if k:
+                    gather_in(k).wait_recv()
             r = mm(xg[kb].reshape(128, 768), wu[kb], NT)
             if k == 0:
                 acc[...] = r
@@ -164,18 +170,20 @@
 
         @pl.when(s == 1)
         def _():
-            hop(u).wait_recv()
+            with scope("hopwait"):
+                hop(u).wait_recv()
             for k in ORDER:
                 gather_cot(u, k).start()
 
         for k in (0, 1, 3, 2):
             kb = lane(4 - k)
-            if k:
-                gather_cot(u, k).wait_recv()
-            else:
-                @pl.when(jnp.logical_not(odd))
-                def _():
-                    cast_down(u, 0).wait_recv()
+            with scope("cotwait"):
+                if k:
+                    gather_cot(u, k).wait_recv()
+                else:
+                    @pl.when(jnp.logical_not(odd))
+                    def _():
+                        cast_down(u, 0).wait_recv()
             r = mm(cg[kb, u], wd[kb], NT)
             if k == 0:
                 acc[0:64, :] = r
@@ -193,7 +201,8 @@
     def finish(u):
         total = cg[l, u].astype(F32) + part[u, 0].astype(F32)
         for k in (1, 3, 2):
-            scatter(u, k).wait_recv()
+            with scope("scatwait"):
+                scatter(u, k).wait_recv()
             total += prs[u, k].astype(F32)
         og[u] = total.astype(BF)
 
@@ -205,8 +214,6 @@
         @pl.when(s == 2)
         def _():
             hop(u).start()
-
-        pltpu.make_async_copy(og.at[u], og_hbm.at[u], out_sem.at[u]).start()
 
     def zcount(t, d):
         return 6 if t == d else 5
@@ -242,20 +249,25 @@
 
     def codes():
         cup[...] = mm(ug[...], proj[0], NN).astype(BF)
-        for t in range(2):
-            make_term(t)
-            ring_start(t)
-
-    first(0)
-    second(0)
-    first(1)
+        with scope("terms"):
+            for t in range(2):
+                make_term(t)
+                ring_start(t)
+
+    with scope("first0"):
+        first(0)
+    with scope("second0"):
+        second(0)
+    with scope("first1"):
+        first(1)
 
     @pl.when(s == 0)
     def _():
         finish(0)
         codes()
 
-    second(1)
+    with scope("second1"):
+        second(1)
 
     @pl.when(s > 0)
     def _():
@@ -269,8 +281,9 @@
         codes()
 
     for k in range(1, 6):
-        for t in range(2):
-            ring_step(t, k)
+        with scope("ringstep"):
+            for t in range(2):
+                ring_step(t, k)
         if k == 3:
             @pl.when(s == 0)
             def _():
@@ -281,26 +294,27 @@
             ysend.at[t, k], yrecv.at[t, k], y_s.at[t, k], y_r.at[t, k], {"dp": ydev(k)}
         )
 
-    for t in range(2):
-        for d in range(2):
-            zcopy(t, d, zcount(t, d) - 1).wait_recv()
-        for k in (3, 2, 1, 0):
-            yo = lax.rem(y + k, 4)
-            r = terms[t, yo, z]
+    with scope("ringlast"):
+        for t in range(2):
             for d in range(2):
-                r += zrecv[t, d, zcount(t, d) - 1, yo].astype(F32)
-            if k:
-                ysend[t, k] = r.astype(BF)
-                ycopy(t, k).start()
-            else:
-                ykeep[t] = r
-
-    outs = []
+                zcopy(t, d, zcount(t, d) - 1).wait_recv()
+            for k in (3, 2, 1, 0):
+                yo = lax.rem(y + k, 4)
+                r = terms[t, yo, z]
+                for d in range(2):
+                    r += zrecv[t, d, zcount(t, d) - 1, yo].astype(F32)
+                if k:
+                    ysend[t, k] = r.astype(BF)
+                    ycopy(t, k).start()
+                else:
+                    ykeep[t] = r
+
     for t in range(2):
         grad = ykeep[t]
-        for k in (1, 2, 3):
-            ycopy(t, k).wait_recv()
-            grad += yrecv[t, k].astype(F32)
+        with scope("ywait"):
+            for k in (1, 2, 3):
+                ycopy(t, k).wait_recv()
+                grad += yrecv[t, k].astype(F32)
         new_first = 0.9 * m1[t] + 0.1 * grad
         new_second = 0.999 * m2[t] + 0.001 * grad * grad
         nfv[t] = new_first
@@ -309,14 +323,7 @@
         high = step.astype(BF)
         low = (step - high.astype(F32)).astype(BF)
         delta = mm(high, proj[t], NT) + mm(low, proj[t], NT)
-        nwv[t] = (base[t] - 0.05 * delta).astype(BF)
-        outs += [
-            pltpu.make_async_copy(nfv.at[t], nf_hbm.at[t], out_sem.at[2 + 3 * t]),
-            pltpu.make_async_copy(nsv.at[t], ns_hbm.at[t], out_sem.at[3 + 3 * t]),
-            pltpu.make_async_copy(nwv.at[t], (nu_hbm, nd_hbm)[t], out_sem.at[4 + 3 * t]),
-        ]
-        for c in outs[-3:]:
-            c.start()
+        (nup, ndown)[t][...] = (base[t] - 0.05 * delta).astype(BF)
 
     @pl.when(s == 3)
     def _():
@@ -350,10 +357,30 @@
         for d in range(2):
             for k in range(zcount(t, d)):
                 zcopy(t, d, k).wait_send()
-    for u in range(2):
-        pltpu.make_async_copy(og.at[u], og_hbm.at[u], out_sem.at[u]).wait()
-    for c in outs:
+
+
+def copy_kernel(*refs):
+    half = len(refs) // 2
+    sems = refs[-1]
+    copies = [
+        pltpu.make_async_copy(refs[i], refs[half + i], sems.at[i]) for i in range(half)
+    ]
+    for c in copies:
+        c.start()
+    for c in copies:
         c.wait()
+
+
+def hand_out(*arrays):
+    return pl.pallas_call(
+        copy_kernel,
+        out_shape=tuple(jax.ShapeDtypeStruct(a.shape, a.dtype) for a in arrays),
+        in_specs=[pl.BlockSpec(memory_space=pl.ANY)] * len(arrays),
+        out_specs=(pl.BlockSpec(memory_space=pl.ANY),) * len(arrays),
+        scratch_shapes=[pltpu.SemaphoreType.DMA((len(arrays),))],
+        compiler_params=pltpu.CompilerParams(vmem_limit_bytes=2 * 2**20),
+        name="hand_out",
+    )(*arrays)
 
 
 def local(zn, inputs, gate_sums, top_grads, up_weight, down_weight, projectors, first_moment, second_moment):
@@ -363,14 +390,14 @@
     og, nf, ns, nu, nd = pl.pallas_call(
         functools.partial(kernel, zn),
         out_shape=(
-            sds((2, 64, 768), BF),
-            sds((2, 64, 128), F32),
-            sds((2, 64, 128), F32),
-            sds((64, 816), BF),
-            sds((64, 816), BF),
+            pltpu.VMEM((2, 64, 768), BF),
+            pltpu.VMEM((2, 64, 128), F32),
+            pltpu.VMEM((2, 64, 128), F32),
+            pltpu.VMEM((64, 816), BF),
+            pltpu.VMEM((64, 816), BF),
         ),
         in_specs=[any_spec] * 8,
-        out_specs=(any_spec,) * 5,
+        out_specs=(pl.BlockSpec(memory_space=pltpu.VMEM),) * 5,
         scratch_shapes=[
             pltpu.VMEM((4, 816, 768), BF),
             pltpu.VMEM((4, 816, 768), BF),
@@ -386,7 +413,6 @@
             pltpu.VMEM((128, 816), BF),
             pltpu.VMEM((2, 4, 64, 768), BF),
             pltpu.VMEM((2, 4, 64, 768), BF),
-            pltpu.VMEM((2, 64, 768), BF),
             pltpu.VMEM((128, 128), BF),
             pltpu.VMEM((128, 128), BF),
             pltpu.VMEM((2, 4, zn, 64, 128), F32),
@@ -396,12 +422,8 @@
             pltpu.VMEM((2, 4, 64, 128), BF),
             pltpu.VMEM((2, 64, 128), F32),
             pltpu.VMEM((2, 64, 816), F32),
-            pltpu.VMEM((2, 64, 128), F32),
-            pltpu.VMEM((2, 64, 128), F32),
-            pltpu.VMEM((2, 64, 816), BF),
             dma((6,)),
             dma((2, 4)),
-            dma((8,)),
             dma((2, 4)),
             dma((2, 4)),
             dma((2, 4)),
@@ -430,6 +452,7 @@
         jnp.swapaxes(first_moment[0, 0], 1, 2),
         jnp.swapaxes(second_moment[0, 0], 1, 2),
     )
+    og, nf, ns, nu, nd = hand_out(og, nf, ns, nu, nd)
     return (
         og[None],
         jnp.swapaxes(nf, 1, 2)[None, None],

time: 118 us -> 110 us (0.932)
  local copies, waits for them, and re-layouts: 7.67 us -> 0 us
    unnamed x5 -> x0, local copies, waits for them, and re-layouts: 7.67 us -> none
    pallas_call x1 -> x2, Pallas kernels: 109 us -> 109 us  [the longest x1 108 us: local(): pl.pallas_call(functools.partial(kernel, zn), out_shape=(pltpu.VMEM((2, 6...]
where the time goes in v2:
time: 110 us
  Pallas kernels  109 us (99%)
    pallas_call x1, Pallas kernels, local(): pl.pallas_call(functools.partial(kernel, zn), out_shape=(pltpu.VMEM((2, 6...  108 us

profile of v2, /device:TPU:6, one launch (start us, length us, event | category | flops | bytes accessed | tf_op | source)
XLA Modules:
  0.0 109.8 jit_solution(4687058485293521700)
XLA Ops:
  0.6 108.3 %relay.1 = (bf16[2,64,768]{2,1,0:T(8,128)(2,1)S(1)}, f32[2,64,128]{2,1,0:T(8,128)S(1)}, f32[2,64,128]{2,1,0:T(8,128)S(1)}, bf16[64,816]{1,0:T(8,128)(2,1)S(1)}, bf16[64,816]{1,0:T(8,128)(2,1)S(1)}) custom-call(bf16[2,64,768]{2,1,0:T(8,128)(2,1)} %bitcast.28, bf16[2,64,816]{2,1,0:T(8,128)(2,1)} %bitcast.27, bf16[2,64,768]{2,1,0:T(8,128)(2,1)} %top_hbm.1, ...), custom_call_target="tpu_custom_call" | custom-call | tf_op jit(solution)/shard_map/relay/pallas_call | solution.py:390
  108.9 0.8 hand_out.1

commit v3 on v2

v3 whole, which is shorter than its diff:
```python
import functools

import jax
import jax.numpy as jnp
from jax import lax
from jax.experimental import pallas as pl
from jax.experimental.pallas import tpu as pltpu
from jax.sharding import PartitionSpec as P

MESH = pl.DeviceIdType.MESH
NT = (((1,), (1,)), ((), ()))
NN = (((1,), (0,)), ((), ()))
TN = (((0,), (0,)), ((), ()))
BF = jnp.bfloat16
F32 = jnp.float32
UNIT = 64


def loop(count, body):
    lax.fori_loop(0, count, lambda i, c: (body(i), c)[1], 0)


def gray(p):
    return p + p // 2 - 2 * (p // 3)


def mm(a, b, dims):
    return lax.dot_general(a, b, dims, preferred_element_type=F32)


def kernel(
    zn,
    x_hbm, gate_hbm, top_hbm, wu_hbm, wd_hbm, proj_hbm, m1_hbm, m2_hbm,
    og, nfv, nsv, nup, ndown,
    wu, wd, proj, gate, m1, m2,
    rows_in, act, acc, ug, hid, part, prs,
    code, terms, zsrc, zrecv, ysend, yrecv, ykeep,
    base,
    loc, wsem,
    ag_s, bc_s, ag_r, yh_s, yh_r, in_s, in_r, rs_s, rs_r, z_s, z_r, y_s, y_r,
):
    xg, cg = rows_in.at[0], rows_in.at[1]
    s = lax.axis_index("segment")
    l = lax.axis_index("lane")
    dp = lax.axis_index("dp")
    z = lax.rem(dp, zn)
    y = dp // zn
    odd = lax.rem(s, 2) == 1
    pair = s + 1 - 2 * lax.rem(s, 2)

    def lane(k):
        return lax.rem(l + k, 4)

    def zdev(k):
        return y * zn + lax.rem(z + k + zn, zn)

    def ydev(k):
        return lax.rem(y + k, 4) * zn + z

    gate_load = pltpu.make_async_copy(gate_hbm, gate, loc.at[0])
    top_load = pltpu.make_async_copy(top_hbm, cg.at[l], loc.at[1])
    late_loads = [
        pltpu.make_async_copy(x_hbm, xg.at[l], loc.at[2]),
        pltpu.make_async_copy(proj_hbm, proj, loc.at[3]),
        pltpu.make_async_copy(m1_hbm, m1, loc.at[4]),
        pltpu.make_async_copy(m2_hbm, m2, loc.at[5]),
    ]
    wd_loads = [
        pltpu.make_async_copy(wd_hbm.at[:, pl.ds(kb * 768, 768)], wd.at[kb], wsem.at[0, kb])
        for kb in range(4)
    ]
    wu_loads = [
        pltpu.make_async_copy(wu_hbm.at[:, pl.ds(kb * 768, 768)], wu.at[kb], wsem.at[1, kb])
        for kb in range(4)
    ]

    @pl.when(s == 3)
    def _():
        top_load.start()

    gate_load.start()
    for c in wd_loads + wu_loads + late_loads:
        c.start()

    barrier = pltpu.get_barrier_semaphore()

    def greet(dev):
        pl.semaphore_signal(barrier, inc=1, device_id=dev, device_id_type=MESH)

    for k in (1, 2, 3):
        greet({"lane": lane(k)})
        greet({"dp": ydev(k)})
    for k in range(4):
        greet({"segment": pair, "lane": lane(k)})
    greet({"segment": 3 - s})
    greet({"dp": zdev(1)})
    greet({"dp": zdev(-1)})
    pl.semaphore_wait(barrier, 13)

    def remote(src, dst, ss, rr, dev):
        return pltpu.make_async_remote_copy(
            src_ref=src, dst_ref=dst, send_sem=ss, recv_sem=rr, device_id=dev, device_id_type=MESH
        )

    def rows(u):
        return pl.ds(pl.multiple_of(u * UNIT, UNIT), UNIT)

    def gather_top(u, k):
        return remote(
            top_hbm.at[rows(u)], cg.at[l, rows(u)], ag_s.at[u, k], ag_r.at[u, k], {"lane": lane(k)}
        )

    def gather_cot(u, k):
        block = cg.at[l, rows(u)]
        return remote(block, block, ag_s.at[u, k], ag_r.at[u, k], {"lane": lane(k)})

    def gather_in(k):
        return remote(x_hbm, xg.at[l], in_s.at[k], in_r.at[k], {"lane": lane(k)})

    def cast_down(u, k):
        return remote(
            og.at[rows(u)],
            cg.at[l, rows(u)],
            bc_s.at[u, k],
            ag_r.at[u, k],
            {"segment": pair, "lane": lane(k)},
        )

    def hop(u):
        return remote(
            og.at[rows(u)], cg.at[l, rows(u)], yh_s.at[u], yh_r.at[u], {"segment": 3 - s}
        )

    def scatter(u, k):
        return remote(
            part.at[k, rows(u)], prs.at[k, rows(u)], rs_s.at[u, k], rs_r.at[u, k], {"lane": lane(k)}
        )

    ORDER = (2, 1, 3)
    count = 128 // UNIT

    @pl.when(s == 3)
    def _():
        for u in range(count):
            for k in ORDER:
                gather_top(u, k).start()

    @pl.when(s < 2)
    def _():
        for k in ORDER:
            gather_in(k).start()

    gate_load.wait()
    v = gate[...].astype(F32)
    act[...] = v / (1.0 + jnp.exp(-v))

    for c in wd_loads + wu_loads:
        c.wait()

    @pl.when(s == 3)
    def _():
        top_load.wait()

    def prep():
        for c in late_loads:
            c.wait()
        acc[...] = jnp.zeros_like(acc)

        def block(p):
            k = gray(p)
            kb = lane(4 - k)

            @pl.when(p > 0)
            def _():
                gather_in(k).wait_recv()

            acc[...] += mm(xg[kb], wu[kb], NT)

        loop(4, block)
        hid[...] = (acc[...] * act[...]).astype(BF)
        code[1] = mm(hid[...], proj[1], NN).astype(BF)

    @pl.when(s < 2)
    def _():
        prep()

    def first(u):
        @pl.when(s == 1)
        def _():
            hop(u).wait_recv()
            for k in ORDER:
                gather_cot(u, k).start()

        acc[0:UNIT, :] = jnp.zeros((UNIT, 816), F32)

        def block(p):
            k = gray(p)
            kb = lane(4 - k)

            @pl.when((p > 0) | jnp.logical_not(odd))
            def _():
                gather_cot(u, k).wait_recv()

            acc[0:UNIT, :] += mm(cg[kb, rows(u)], wd[kb], NT)

        loop(4, block)
        ug[rows(u), :] = (acc[0:UNIT, :] * act[rows(u), :]).astype(BF)

    def second(u):
        def block(p):
            k = gray(3 - p)
            part[k, rows(u)] = mm(ug[rows(u), :], wu[lane(k)], NN).astype(BF)

            @pl.when(k > 0)
            def _():
                scatter(u, k).start()

        loop(4, block)

    def finish(u):
        total = cg[l, rows(u)].astype(F32) + part[0, rows(u)].astype(F32)
        for k in (1, 3, 2):
            scatter(u, k).wait_recv()
            total += prs[k, rows(u)].astype(F32)
        og[rows(u)] = total.astype(BF)

        @pl.when(odd)
        def _():
            for k in (2, 1, 3, 0):
                cast_down(u, k).start()

        @pl.when(s == 2)
        def _():
            hop(u).start()

    def chain(c):
        t, d, h = c // 4, lax.rem(c // 2, 2), lax.rem(c, 2)
        steps = 5 + lax.rem(t + d + 1, 2)
        return t, d, h, steps

    def zcopy(c, k, src):
        d = lax.rem(c // 2, 2)
        return remote(
            src, zrecv.at[c, k], z_s.at[c, k], z_r.at[c, k], {"dp": zdev(2 * d - 1)}
        )

    def local_term(c, k):
        t, d, h, steps = chain(c)
        to = lax.rem(z + (2 * d - 1) * (steps - k) + zn, zn)
        return terms[t, pl.ds(2 * h, 2), to]

    def codes():
        code[0] = mm(ug[...], proj[0], NN).astype(BF)
        for t in range(2):
            def term(kb):
                r = mm(rows_in[t, kb], code[t], TN)
                terms[t, kb] = r.reshape(zn, 64, 128)

            loop(4, term)

            def start(i):
                c = 4 * t + i
                zsrc[c] = local_term(c, 0).astype(BF)
                zcopy(c, 0, zsrc.at[c]).start()

            loop(4, start)

    last = count - 1

    def unit(u):
        first(u)

        @pl.when((u == last) & (s == 0))
        def _():
            codes()

        second(u)

        @pl.when(u > 0)
        def _():
            finish(u - 1)

    loop(count, unit)

    @pl.when(s > 0)
    def _():
        finish(last)

        @pl.when(s > 1)
        def _():
            for k in ORDER:
                gather_in(k).start()
            prep()

        codes()

    pick = lax.broadcasted_iota(jnp.int32, (64, 128), 0) + 64 * lax.rem(z, 2)
    pick = (lax.broadcasted_iota(jnp.int32, (64, 128), 1) == pick).astype(BF)
    at = pl.ds(pl.multiple_of((z // 2) * 128, 128), 128)
    base[0] = mm(pick, wu[y, :, at], NT)
    base[1] = mm(pick, wd[y, :, at], NT)

    def ring_step(i):
        k = i + 1

        def move(c):
            steps = chain(c)[3]

            @pl.when(k < steps)
            def _():
                held = zrecv.at[c, k - 1]
                zcopy(c, k - 1, held).wait_recv()
                zrecv[c, k - 1] = (held[...].astype(F32) + local_term(c, k)).astype(BF)
                zcopy(c, k, held).start()

        loop(8, move)

        @pl.when((k == 2) & (s == 0))
        def _():
            finish(last)

    loop(5, ring_step)

    def ycopy(t, k):
        return remote(
            ysend.at[t, k], yrecv.at[t, k], y_s.at[t, k], y_r.at[t, k], {"dp": ydev(k)}
        )

    for t in range(2):
        for i in range(4):
            c = 4 * t + i
            zcopy(c, 4 if i // 2 != t else 5, zrecv.at[c, 0]).wait_recv()

        def share(i):
            k = 3 - i
            yo = lax.rem(y + k, 4)
            r = terms[t, yo, z]
            for d in range(2):
                c = (t * 2 + d) * 2 + yo // 2
                r += zrecv[c, 5 if t == d else 4, lax.rem(yo, 2)].astype(F32)

            @pl.when(k > 0)
            def _():
                ysend[t, k] = r.astype(BF)
                ycopy(t, k).start()

            @pl.when(k == 0)
            def _():
                ykeep[t] = r

        loop(4, share)

    for t in range(2):
        grad = ykeep[t]
        for k in (1, 2, 3):
            ycopy(t, k).wait_recv()
            grad += yrecv[t, k].astype(F32)
        new_first = 0.9 * m1[t] + 0.1 * grad
        new_second = 0.999 * m2[t] + 0.001 * grad * grad
        nfv[t] = new_first
        nsv[t] = new_second
        step = new_first / (jnp.sqrt(new_second) + 1e-08)
        high = step.astype(BF)
        low = (step - high.astype(F32)).astype(BF)
        delta = mm(high, proj[t], NT) + mm(low, proj[t], NT)
        (nup, ndown)[t][...] = (base[t] - 0.05 * delta).astype(BF)

    def drain_unit(u):
        @pl.when(s == 3)
        def _():
            for k in ORDER:
                gather_top(u, k).wait_send()

        @pl.when(s == 1)
        def _():
            for k in ORDER:
                gather_cot(u, k).wait_send()

        @pl.when(odd)
        def _():
            for k in range(4):
                cast_down(u, k).wait_send()

        @pl.when(s == 2)
        def _():
            hop(u).wait_send()

        for k in ORDER:
            scatter(u, k).wait_send()

    loop(count, drain_unit)
    for k in ORDER:
        gather_in(k).wait_send()
        for t in range(2):
            ycopy(t, k).wait_send()
    def drain(c):
        def sent(k):
            zcopy(c, k, zsrc.at[c]).wait_send()

        loop(5, sent)

        @pl.when(chain(c)[3] == 6)
        def _():
            sent(5)

    loop(8, drain)


def copy_kernel(*refs):
    half = len(refs) // 2
    sems = refs[-1]
    copies = [
        pltpu.make_async_copy(refs[i], refs[half + i], sems.at[i]) for i in range(half)
    ]
    for c in copies:
        c.start()
    for c in copies:
        c.wait()


def hand_out(*arrays):
    return pl.pallas_call(
        copy_kernel,
        out_shape=tuple(jax.ShapeDtypeStruct(a.shape, a.dtype) for a in arrays),
        in_specs=[pl.BlockSpec(memory_space=pl.ANY)] * len(arrays),
        out_specs=(pl.BlockSpec(memory_space=pl.ANY),) * len(arrays),
        scratch_shapes=[pltpu.SemaphoreType.DMA((len(arrays),))],
        compiler_params=pltpu.CompilerParams(vmem_limit_bytes=2 * 2**20),
        name="hand_out",
    )(*arrays)


def local(zn, inputs, gate_sums, top_grads, up_weight, down_weight, projectors, first_moment, second_moment):
    sds = jax.ShapeDtypeStruct
    any_spec = pl.BlockSpec(memory_space=pl.ANY)
    dma = pltpu.SemaphoreType.DMA
    count = 128 // UNIT
    og, nf, ns, nu, nd = pl.pallas_call(
        functools.partial(kernel, zn),
        out_shape=(
            pltpu.VMEM((128, 768), BF),
            pltpu.VMEM((2, 64, 128), F32),
            pltpu.VMEM((2, 64, 128), F32),
            pltpu.VMEM((64, 816), BF),
            pltpu.VMEM((64, 816), BF),
        ),
        in_specs=[any_spec] * 8,
        out_specs=(pl.BlockSpec(memory_space=pltpu.VMEM),) * 5,
        scratch_shapes=[
            pltpu.VMEM((4, 816, 768), BF),
            pltpu.VMEM((4, 816, 768), BF),
            pltpu.VMEM((2, 816, 128), BF),
            pltpu.VMEM((128, 816), BF),
            pltpu.VMEM((2, 64, 128), F32),
            pltpu.VMEM((2, 64, 128), F32),
            pltpu.VMEM((2, 4, 128, 768), BF),
            pltpu.VMEM((128, 816), F32),
            pltpu.VMEM((128, 816), F32),
            pltpu.VMEM((128, 816), BF),
            pltpu.VMEM((128, 816), BF),
            pltpu.VMEM((4, 128, 768), BF),
            pltpu.VMEM((4, 128, 768), BF),
            pltpu.VMEM((2, 128, 128), BF),
            pltpu.VMEM((2, 4, zn, 64, 128), F32),
            pltpu.VMEM((8, 2, 64, 128), BF),
            pltpu.VMEM((8, 6, 2, 64, 128), BF),
            pltpu.VMEM((2, 4, 64, 128), BF),
            pltpu.VMEM((2, 4, 64, 128), BF),
            pltpu.VMEM((2, 64, 128), F32),
            pltpu.VMEM((2, 64, 816), F32),
            dma((6,)),
            dma((2, 4)),
            dma((count, 4)),
            dma((count, 4)),
            dma((count, 4)),
            dma((count,)),
            dma((count,)),
            dma((4,)),
            dma((4,)),
            dma((count, 4)),
            dma((count, 4)),
            dma((8, 6)),
            dma((8, 6)),
            dma((2, 4)),
            dma((2, 4)),
        ],
        compiler_params=pltpu.CompilerParams(
            collective_id=0, has_side_effects=True, vmem_limit_bytes=60 * 2**20
        ),
        name="relay",
    )(
        inputs[0].reshape(128, 768),
        gate_sums[0].reshape(128, 816),
        top_grads.reshape(128, 768),
        jnp.swapaxes(up_weight[0], 0, 1),
        down_weight[0],
        projectors[0],
        jnp.swapaxes(first_moment[0, 0], 1, 2),
        jnp.swapaxes(second_moment[0, 0], 1, 2),
    )
    og, nf, ns, nu, nd = hand_out(og, nf, ns, nu, nd)
    return (
        og.reshape(1, 2, 64, 768),
        jnp.swapaxes(nf, 1, 2)[None, None],
        jnp.swapaxes(ns, 1, 2)[None, None],
        nu[None],
        jnp.swapaxes(nd, 0, 1)[None],
    )


def solution(mesh):
    placed = (
        P("segment", None, "dp", "lane"),
        P("segment", None, "dp", "lane"),
        P(None, "dp", "lane"),
        P("segment", None, "lane"),
        P("segment", "lane", None),
        P("segment", None, "lane", None),
        P("segment", "lane", None, None, "dp"),
        P("segment", "lane", None, None, "dp"),
    )
    return jax.shard_map(
        functools.partial(local, mesh.shape["dp"] // 4),
        mesh=mesh,
        in_specs=placed,
        out_specs=(
            P("segment", None, "dp", "lane"),
            P("segment", "lane", None, None, "dp"),
            P("segment", "lane", None, None, "dp"),
            P("segment", "dp", "lane"),
            P("segment", "lane", "dp"),
        ),
        check_vma=False,
    )
```

time: 110 us -> 104 us (0.945)
  Pallas kernels: 109 us -> 102 us
    pallas_call x1, Pallas kernels: 108 us -> 102 us  [local(): pl.pallas_call(functools.partial(kernel, zn), out_shape=(pltpu.VMEM((128,...]
where the time goes in v3:
time: 104 us; the launch traced here: 103 us
  Pallas kernels  102 us (98%)
    pallas_call x1, Pallas kernels, local(): pl.pallas_call(functools.partial(kernel, zn), out_shape=(pltpu.VMEM((128,...  102 us

profile of v3, /device:TPU:6, one launch (start us, length us, event | category | flops | bytes accessed | tf_op | source)
XLA Modules:
  0.0 103.1 jit_solution(12091649008052506569)
XLA Ops:
  0.6 101.6 %relay.1 = (bf16[128,768]{1,0:T(8,128)(2,1)S(1)}, f32[2,64,128]{2,1,0:T(8,128)S(1)}, f32[2,64,128]{2,1,0:T(8,128)S(1)}, bf16[64,816]{1,0:T(8,128)(2,1)S(1)}, bf16[64,816]{1,0:T(8,128)(2,1)S(1)}) custom-call(bf16[128,768]{1,0:T(8,128)(2,1)} %bitcast.29, bf16[128,816]{1,0:T(8,128)(2,1)} %bitcast.28, bf16[128,768]{1,0:T(8,128)(2,1)} %bitcast.30, ...), custom_call_target="tpu_custom_call" | custom-call | tf_op jit(solution)/shard_map/relay/pallas_call | solution.py:438
  102.2 0.8 hand_out.1

commit v4 on v3

--- a/solution.py
+++ b/solution.py
@@ -35,9 +35,9 @@
     wu, wd, proj, gate, m1, m2,
     rows_in, act, acc, ug, hid, part, prs,
     code, terms, zsrc, zrecv, ysend, yrecv, ykeep,
-    base,
+    base, proj2, turned,
     loc, wsem,
-    ag_s, bc_s, ag_r, yh_s, yh_r, in_s, in_r, rs_s, rs_r, z_s, z_r, y_s, y_r,
+    ag_s, bc_s, ag_r, yh_s, yh_r, in_s, in_r, rs_s, rs_r, z_s, z_r, y_s, y_r, turn,
 ):
     xg, cg = rows_in.at[0], rows_in.at[1]
     s = lax.axis_index("segment")
@@ -110,8 +110,11 @@
             top_hbm.at[rows(u)], cg.at[l, rows(u)], ag_s.at[u, k], ag_r.at[u, k], {"lane": lane(k)}
         )
 
-    def gather_cot(u, k):
-        block = cg.at[l, rows(u)]
+    def half(u, h):
+        return pl.ds(pl.multiple_of(u * UNIT + h * (UNIT // 2), UNIT // 2), UNIT // 2)
+
+    def gather_cot(u, k, span=None):
+        block = cg.at[l, rows(u) if span is None else span]
         return remote(block, block, ag_s.at[u, k], ag_r.at[u, k], {"lane": lane(k)})
 
     def gather_in(k):
@@ -126,9 +129,9 @@
             {"segment": pair, "lane": lane(k)},
         )
 
-    def hop(u):
+    def hop(u, h):
         return remote(
-            og.at[rows(u)], cg.at[l, rows(u)], yh_s.at[u], yh_r.at[u], {"segment": 3 - s}
+            og.at[half(u, h)], cg.at[l, half(u, h)], yh_s.at[u, h], yh_r.at[u, h], {"segment": 3 - s}
         )
 
     def scatter(u, k):
@@ -136,14 +139,13 @@
             part.at[k, rows(u)], prs.at[k, rows(u)], rs_s.at[u, k], rs_r.at[u, k], {"lane": lane(k)}
         )
 
-    ORDER = (2, 1, 3)
+    ORDER = (1, 3, 2)
     count = 128 // UNIT
 
     @pl.when(s == 3)
     def _():
-        for u in range(count):
-            for k in ORDER:
-                gather_top(u, k).start()
+        for k in ORDER:
+            gather_top(0, k).start()
 
     @pl.when(s < 2)
     def _():
@@ -159,6 +161,9 @@
 
     @pl.when(s == 3)
     def _():
+        for u in range(1, count):
+            for k in ORDER:
+                gather_top(u, k).start()
         top_load.wait()
 
     def prep():
@@ -184,12 +189,20 @@
     def _():
         prep()
 
+    @pl.when(s < 3)
+    def _():
+        def turn_block(kb):
+            turned[kb] = wd[kb].T
+
+        loop(4, turn_block)
+
     def first(u):
         @pl.when(s == 1)
         def _():
-            hop(u).wait_recv()
-            for k in ORDER:
-                gather_cot(u, k).start()
+            for h in range(2):
+                hop(u, h).wait_recv()
+                for k in ORDER:
+                    gather_cot(u, k, half(u, h)).start()
 
         acc[0:UNIT, :] = jnp.zeros((UNIT, 816), F32)
 
@@ -201,7 +214,13 @@
             def _():
                 gather_cot(u, k).wait_recv()
 
-            acc[0:UNIT, :] += mm(cg[kb, rows(u)], wd[kb], NT)
+            @pl.when(s == 3)
+            def _():
+                acc[0:UNIT, :] += mm(cg[kb, rows(u)], wd[kb], NT)
+
+            @pl.when(s < 3)
+            def _():
+                acc[0:UNIT, :] += mm(cg[kb, rows(u)], turned[kb], NN)
 
         loop(4, block)
         ug[rows(u), :] = (acc[0:UNIT, :] * act[rows(u), :]).astype(BF)
@@ -226,12 +245,13 @@
 
         @pl.when(odd)
         def _():
-            for k in (2, 1, 3, 0):
+            for k in (0, 1, 3, 2):
                 cast_down(u, k).start()
 
         @pl.when(s == 2)
         def _():
-            hop(u).start()
+            for h in range(2):
+                hop(u, h).start()
 
     def chain(c):
         t, d, h = c // 4, lax.rem(c // 2, 2), lax.rem(c, 2)
@@ -286,6 +306,14 @@
     def _():
         finish(last)
 
+        @pl.when(s == 2)
+        def _():
+            pl.semaphore_signal(turn, inc=1, device_id={"segment": 3}, device_id_type=MESH)
+
+        @pl.when(s == 3)
+        def _():
+            pl.semaphore_wait(turn, 1)
+
         @pl.when(s > 1)
         def _():
             for k in ORDER:
@@ -293,12 +321,6 @@
             prep()
 
         codes()
-
-    pick = lax.broadcasted_iota(jnp.int32, (64, 128), 0) + 64 * lax.rem(z, 2)
-    pick = (lax.broadcasted_iota(jnp.int32, (64, 128), 1) == pick).astype(BF)
-    at = pl.ds(pl.multiple_of((z // 2) * 128, 128), 128)
-    base[0] = mm(pick, wu[y, :, at], NT)
-    base[1] = mm(pick, wd[y, :, at], NT)
 
     def ring_step(i):
         k = i + 1
@@ -314,10 +336,6 @@
                 zcopy(c, k, held).start()
 
         loop(8, move)
-
-        @pl.when((k == 2) & (s == 0))
-        def _():
-            finish(last)
 
     loop(5, ring_step)
 
@@ -349,6 +367,18 @@
                 ykeep[t] = r
 
         loop(4, share)
+
+    pick = lax.broadcasted_iota(jnp.int32, (64, 128), 0) + 64 * lax.rem(z, 2)
+    pick = (lax.broadcasted_iota(jnp.int32, (64, 128), 1) == pick).astype(BF)
+    at = pl.ds(pl.multiple_of((z // 2) * 128, 128), 128)
+    proj2[:, :, 0:128] = proj[...]
+    proj2[:, :, 128:256] = proj[...]
+    base[0] = mm(pick, wu[y, :, at], NT)
+    base[1] = mm(pick, wd[y, :, at], NT)
+
+    @pl.when(s == 0)
+    def _():
+        finish(last)
 
     for t in range(2):
         grad = ykeep[t]
@@ -362,7 +392,7 @@
         step = new_first / (jnp.sqrt(new_second) + 1e-08)
         high = step.astype(BF)
         low = (step - high.astype(F32)).astype(BF)
-        delta = mm(high, proj[t], NT) + mm(low, proj[t], NT)
+        delta = mm(jnp.concatenate([high, low], axis=1), proj2[t], NT)
         (nup, ndown)[t][...] = (base[t] - 0.05 * delta).astype(BF)
 
     def drain_unit(u):
@@ -383,7 +413,8 @@
 
         @pl.when(s == 2)
         def _():
-            hop(u).wait_send()
+            for h in range(2):
+                hop(u, h).wait_send()
 
         for k in ORDER:
             scatter(u, k).wait_send()
@@ -468,13 +499,15 @@
             pltpu.VMEM((2, 4, 64, 128), BF),
             pltpu.VMEM((2, 64, 128), F32),
             pltpu.VMEM((2, 64, 816), F32),
+            pltpu.VMEM((2, 816, 256), BF),
+            pltpu.VMEM((4, 768, 816), BF),
             dma((6,)),
             dma((2, 4)),
             dma((count, 4)),
             dma((count, 4)),
             dma((count, 4)),
-            dma((count,)),
-            dma((count,)),
+            dma((count, 2)),
+            dma((count, 2)),
             dma((4,)),
             dma((4,)),
             dma((count, 4)),
@@ -483,6 +516,7 @@
             dma((8, 6)),
             dma((2, 4)),
             dma((2, 4)),
+            pltpu.SemaphoreType.REGULAR,
         ],
         compiler_params=pltpu.CompilerParams(
             collective_id=0, has_side_effects=True, vmem_limit_bytes=60 * 2**20

time: 104 us -> 98.1 us (0.943)
  Pallas kernels: 102 us -> 97.3 us
    pallas_call x1, Pallas kernels: 102 us -> 96.5 us  [local(): pl.pallas_call(functools.partial(kernel, zn), out_shape=(pltpu.VMEM((128,...]
where the time goes in v4:
time: 98.1 us; the launch traced here: 97.9 us
  Pallas kernels  97.3 us (99%)
    pallas_call x1, Pallas kernels, local(): pl.pallas_call(functools.partial(kernel, zn), out_shape=(pltpu.VMEM((128,...  96.5 us

profile of v4, /device:TPU:6, one launch (start us, length us, event | category | flops | bytes accessed | tf_op | source)
XLA Modules:
  0.0 97.9 jit_solution(10396777792237002430)
XLA Ops:
  0.6 96.5 %relay.1 = (bf16[128,768]{1,0:T(8,128)(2,1)S(1)}, f32[2,64,128]{2,1,0:T(8,128)S(1)}, f32[2,64,128]{2,1,0:T(8,128)S(1)}, bf16[64,816]{1,0:T(8,128)(2,1)S(1)}, bf16[64,816]{1,0:T(8,128)(2,1)S(1)}) custom-call(bf16[128,768]{1,0:T(8,128)(2,1)} %bitcast.29, bf16[128,816]{1,0:T(8,128)(2,1)} %bitcast.28, bf16[128,768]{1,0:T(8,128)(2,1)} %bitcast.30, ...), custom_call_target="tpu_custom_call" | custom-call | tf_op jit(solution)/shard_map/relay/pallas_call | solution.py:469
  97.1 0.8 hand_out.1

commit v5 on v4

--- a/solution.py
+++ b/solution.py
@@ -92,10 +92,15 @@
         greet({"dp": ydev(k)})
     for k in range(4):
         greet({"segment": pair, "lane": lane(k)})
-    greet({"segment": 3 - s})
+    across = (s == 1) | (s == 2)
+
+    @pl.when(across)
+    def _():
+        greet({"segment": 3 - s})
+
     greet({"dp": zdev(1)})
     greet({"dp": zdev(-1)})
-    pl.semaphore_wait(barrier, 13)
+    pl.semaphore_wait(barrier, 12 + across.astype(jnp.int32))
 
     def remote(src, dst, ss, rr, dev):
         return pltpu.make_async_remote_copy(
@@ -156,9 +161,6 @@
     v = gate[...].astype(F32)
     act[...] = v / (1.0 + jnp.exp(-v))
 
-    for c in wd_loads + wu_loads:
-        c.wait()
-
     @pl.when(s == 3)
     def _():
         for u in range(1, count):
@@ -166,6 +168,16 @@
                 gather_top(u, k).start()
         top_load.wait()
 
+    for c in wd_loads:
+        c.wait()
+
+    def turn_block(kb):
+        turned[kb] = wd[kb].T
+
+    loop(4, turn_block)
+    for c in wu_loads:
+        c.wait()
+
     def prep():
         for c in late_loads:
             c.wait()
@@ -189,13 +201,6 @@
     def _():
         prep()
 
-    @pl.when(s < 3)
-    def _():
-        def turn_block(kb):
-            turned[kb] = wd[kb].T
-
-        loop(4, turn_block)
-
     def first(u):
         @pl.when(s == 1)
         def _():
@@ -214,13 +219,7 @@
             def _():
                 gather_cot(u, k).wait_recv()
 
-            @pl.when(s == 3)
-            def _():
-                acc[0:UNIT, :] += mm(cg[kb, rows(u)], wd[kb], NT)
-
-            @pl.when(s < 3)
-            def _():
-                acc[0:UNIT, :] += mm(cg[kb, rows(u)], turned[kb], NN)
+            acc[0:UNIT, :] += mm(cg[kb, rows(u)], turned[kb], NN)
 
         loop(4, block)
         ug[rows(u), :] = (acc[0:UNIT, :] * act[rows(u), :]).astype(BF)

time: 98.1 us -> 97 us (0.989)
  Pallas kernels: 97.3 us -> 96.3 us
    pallas_call x1, Pallas kernels: 96.5 us -> 95.4 us  [local(): pl.pallas_call(functools.partial(kernel, zn), out_shape=(pltpu.VMEM((128,...]
where the time goes in v5:
time: 97 us; the launch traced here: 96.9 us
  Pallas kernels  96.3 us (99%)
    pallas_call x1, Pallas kernels, local(): pl.pallas_call(functools.partial(kernel, zn), out_shape=(pltpu.VMEM((128,...  95.4 us

profile of v5, /device:TPU:6, one launch (start us, length us, event | category | flops | bytes accessed | tf_op | source)
XLA Modules:
  0.0 96.9 jit_solution(6194887255580878830)
XLA Ops:
  0.6 95.4 %relay.1 = (bf16[128,768]{1,0:T(8,128)(2,1)S(1)}, f32[2,64,128]{2,1,0:T(8,128)S(1)}, f32[2,64,128]{2,1,0:T(8,128)S(1)}, bf16[64,816]{1,0:T(8,128)(2,1)S(1)}, bf16[64,816]{1,0:T(8,128)(2,1)S(1)}) custom-call(bf16[128,768]{1,0:T(8,128)(2,1)} %bitcast.29, bf16[128,816]{1,0:T(8,128)(2,1)} %bitcast.28, bf16[128,768]{1,0:T(8,128)(2,1)} %bitcast.30, ...), custom_call_target="tpu_custom_call" | custom-call | tf_op jit(solution)/shard_map/relay/pallas_call | solution.py:468
  96.1 0.8 hand_out.1

commit v6 on v5

--- a/solution.py
+++ b/solution.py
@@ -275,14 +275,15 @@
                 r = mm(rows_in[t, kb], code[t], TN)
                 terms[t, kb] = r.reshape(zn, 64, 128)
 
-            loop(4, term)
-
-            def start(i):
-                c = 4 * t + i
-                zsrc[c] = local_term(c, 0).astype(BF)
-                zcopy(c, 0, zsrc.at[c]).start()
-
-            loop(4, start)
+            def half_term(h):
+                term(2 * h)
+                term(2 * h + 1)
+                for d in range(2):
+                    c = 4 * t + 2 * d + h
+                    zsrc[c] = local_term(c, 0).astype(BF)
+                    zcopy(c, 0, zsrc.at[c]).start()
+
+            loop(2, half_term)
 
     last = count - 1
 

time: 97 us -> 96.4 us (level)
  no operation moved by 1% of the time
where the time goes in v6:
time: 96.4 us; the launch traced here: 96.2 us
  Pallas kernels  95.6 us (99%)
    pallas_call x1, Pallas kernels, local(): pl.pallas_call(functools.partial(kernel, zn), out_shape=(pltpu.VMEM((128,...  94.8 us

profile of v6, /device:TPU:6, one launch (start us, length us, event | category | flops | bytes accessed | tf_op | source)
XLA Modules:
  0.0 96.2 jit_solution(8216518340131601492)
XLA Ops:
  0.6 94.8 %relay.1 = (bf16[128,768]{1,0:T(8,128)(2,1)S(1)}, f32[2,64,128]{2,1,0:T(8,128)S(1)}, f32[2,64,128]{2,1,0:T(8,128)S(1)}, bf16[64,816]{1,0:T(8,128)(2,1)S(1)}, bf16[64,816]{1,0:T(8,128)(2,1)S(1)}) custom-call(bf16[128,768]{1,0:T(8,128)(2,1)} %bitcast.29, bf16[128,816]{1,0:T(8,128)(2,1)} %bitcast.28, bf16[128,768]{1,0:T(8,128)(2,1)} %bitcast.30, ...), custom_call_target="tpu_custom_call" | custom-call | tf_op jit(solution)/shard_map/relay/pallas_call | solution.py:469
  95.4 0.8 hand_out.1
